TPU v7x, 512 devices: a whole 4x8x8 slice. The times are simulated.
512 devices in a mesh: tok: 16 (over x, z_hi, core), feat: 32 (over y, z_lo).
Axes of the slice: x: 4, y: 8, z: 8 (z_hi: 2, z_lo: 4; z = z_hi * 4 + z_lo), core: 2. Of those that a mesh axis runs over, the one named last changes fastest.
Arguments:
- tokens: bfloat16 [16384, 16384], P('tok', 'feat'), parts along dimension 0, may hold values from -6 to 6
- butterfly: bfloat16 [6, 512, 16384], P(None, None, 'feat'), may hold values from -0.109375 to 0.109375
- rank_down: bfloat16 [16384, 512], P('feat'), may hold values from -0.046875 to 0.046875
- rank_up: bfloat16 [512, 16384], P(None, 'feat'), may hold values from -0.25 to 0.25
Outputs:
- mixed: bfloat16 [16384, 16384], P('tok', 'feat'), parts along dimension 0
There are 16 independent parts, one for each index of `tok`. A program takes and returns all parts, laid end to end along the dimension named above; an argument that names none is the same for every part. Nothing has to cross between parts.
All inputs are finite; a program needn't handle non-finite values.
Results may differ from a plain program's by a relative error of at most 0.004.
Values may be sent and summed in bfloat16 or wider, within the bound.
A program may use at most 64 MiB of HBM per device.

v0:
```python
import jax
import jax.numpy as jnp
from jax import lax
from jax.sharding import PartitionSpec as P


def in_blocks(value, dim, peers):
    dims = value.shape
    pieces = value.reshape(*dims[:dim], peers, dims[dim] // peers, *dims[dim + 1 :])
    return jnp.moveaxis(pieces, dim, 0)


def sent_and_summed(value, axis, dim):
    peers = lax.axis_size(axis)
    pieces = lax.all_to_all(in_blocks(value, dim, peers), axis, 0, 0, tiled=True)
    return jnp.sum(pieces, axis=0)


def joined_along(pieces, dim):
    pieces = jnp.moveaxis(pieces, 0, dim)
    dims = pieces.shape
    return pieces.reshape(*dims[:dim], dims[dim] * dims[dim + 1], *dims[dim + 2 :])


def copy_for_each(value, axis):
    copies = jnp.broadcast_to(value, (lax.axis_size(axis), *value.shape))
    return lax.all_to_all(copies, axis, split_axis=0, concat_axis=0, tiled=True)


def collect(value, axis, dim):
    return joined_along(copy_for_each(value, axis), dim)


def from_partner(value, axis, apart):
    return lax.ppermute(value, axis, [(i, i ^ 1 << apart) for i in range(lax.axis_size(axis))])


def shards(tokens, butterfly, rank_down, rank_up):
    levels = lax.axis_size("feat").bit_length() - 1
    rank_part = sent_and_summed(
        jnp.dot(tokens, rank_down, preferred_element_type=jnp.float32), "feat", 1
    ).astype(jnp.bfloat16)
    rank_mid = collect(rank_part, "feat", 1)
    sparse = jnp.dot(tokens, butterfly[0], preferred_element_type=jnp.float32)
    for level in range(levels):
        neighbour = from_partner(tokens, "feat", level)
        sparse = sparse + jnp.dot(
            neighbour, butterfly[level + 1], preferred_element_type=jnp.float32
        )
    dense = sparse + jnp.dot(rank_mid, rank_up, preferred_element_type=jnp.float32)
    return jax.nn.gelu(dense, approximate=False).astype(jnp.bfloat16)


def solution(mesh):
    return jax.shard_map(
        shards,
        mesh=mesh,
        in_specs=(P("tok", "feat"), P(None, None, "feat"), P("feat", None), P(None, "feat")),
        out_specs=P("tok", "feat"),
        check_vma=False,
    )
```

profile of v0, /device:TPU:14, one launch (start us, length us, event | category | flops | bytes accessed | tf_op | source)
XLA Modules:
  0.0 214.0 jit_solution(2971480655030910863)
XLA Ops:
  0.0 0.0 copy-start
  0.0 1.0 copy-done
  1.0 3.3 %fusion.30 = f32[1024,512]{0,1:T(8,128)} fusion(bf16[1024,512]{1,0:T(8,128)(2,1)} %param.4, bf16[512,512]{1,0:T(8,128)(2,1)S(1)} %copy-done), kind=kOutput, calls=%fused_computation.38 | convolution fusion | flops 536870912 | bytes 3670016 | tf_op jit(solution)/shard_map/dot_general | solution.py:41
  4.4 13.1 %all-to-all-start = ((f32[32,1024,16]{1,2,0:T(8,128)}), f32[32,1024,16]{1,2,0:T(8,128)S(1)}, u32[]{:S(2)}, u32[]{:S(2)}) async-start(f32[32,1024,16]{1,2,0:T(8,128)} %bitcast.7), calls=%async_computation | async-start | bytes 4194304 | tf_op jit(solution)/shard_map/all_to_all | solution.py:15
  17.5 4.3 %collective-permute-start.3 = (bf16[1024,512]{1,0:T(8,128)(2,1)}, bf16[1024,512]{1,0:T(8,128)(2,1)}, u32[]{:S(2)}, u32[]{:S(2)}) collective-permute-start(bf16[1024,512]{1,0:T(8,128)(2,1)} %param.4), channel_id=1, source_target_pairs={{0,8},{1,9},{2,10},{3,11},{4,12},{5,13},{6,14},{7,15},{8,0},{9,1},... | collective-permute-start | bytes 3145736 | tf_op jit(solution)/shard_map/ppermute | solution.py:35
  21.8 63.4 %all-to-all-done = f32[32,1024,16]{1,2,0:T(8,128)S(1)} async-done(((f32[32,1024,16]{1,2,0:T(8,128)}), f32[32,1024,16]{1,2,0:T(8,128)S(1)}, u32[]{:S(2)}, u32[]{:S(2)}) %all-to-all-start) | async-done | bytes 2097184 | tf_op jit(solution)/shard_map/all_to_all | solution.py:15
  85.2 0.1 reduce_sum.9
  85.3 0.0 copy-start.1
  85.3 1.1 broadcast_in_dim.3
  86.4 13.2 %all-to-all-start.1 = ((bf16[32,1024,16]{1,2,0:T(8,128)(2,1)}), bf16[32,1024,16]{1,2,0:T(8,128)(2,1)S(1)}, u32[]{:S(2)}, u32[]{:S(2)}) async-start(bf16[32,1024,16]{1,2,0:T(8,128)(2,1)} %broadcast_in_dim.3), calls=%async_computation.1 | async-start | bytes 2097152 | tf_op jit(solution)/shard_map/all_to_all | solution.py:27
  99.6 0.0 copy-done.1
  99.6 0.0 copy-start.2
  99.7 2.4 %collective-permute-start.2 = (bf16[1024,512]{1,0:T(8,128)(2,1)S(1)}, bf16[1024,512]{1,0:T(8,128)(2,1)S(1)}, u32[]{:S(2)}, u32[]{:S(2)}) collective-permute-start(bf16[1024,512]{1,0:T(8,128)(2,1)S(1)} %copy-done.1), channel_id=1, source_target_pairs={{0,4},{1,5},{2,6},{3,7},{4,0},{5,1},{6,2},{7,3},{8,12},{9,13},{10,... | collective-permute-start | bytes 3145736 | tf_op jit(solution)/shard_map/ppermute | solution.py:35
  102.1 4.6 %collective-permute-start.1 = (bf16[1024,512]{1,0:T(8,128)(2,1)S(1)}, bf16[1024,512]{1,0:T(8,128)(2,1)S(1)}, u32[]{:S(2)}, u32[]{:S(2)}) collective-permute-start(bf16[1024,512]{1,0:T(8,128)(2,1)S(1)} %copy-done.1), channel_id=1, source_target_pairs={{0,2},{1,3},{2,0},{3,1},{4,6},{5,7},{6,4},{7,5},{8,10},{9,11},{10,... | collective-permute-start | bytes 3145736 | tf_op jit(solution)/shard_map/ppermute | solution.py:35
  106.7 3.4 %collective-permute-start = (bf16[1024,512]{1,0:T(8,128)(2,1)S(1)}, bf16[1024,512]{1,0:T(8,128)(2,1)S(1)}, u32[]{:S(2)}, u32[]{:S(2)}) collective-permute-start(bf16[1024,512]{1,0:T(8,128)(2,1)S(1)} %copy-done.1), channel_id=1, source_target_pairs={{0,1},{1,0},{2,3},{3,2},{4,5},{5,4},{6,7},{7,6},{8,9},{9,8},{10,11... | collective-permute-start | bytes 3145736 | tf_op jit(solution)/shard_map/ppermute | solution.py:35
  110.1 7.3 %collective-permute-start.4 = (bf16[1024,512]{1,0:T(8,128)(2,1)S(1)}, bf16[1024,512]{1,0:T(8,128)(2,1)}, u32[]{:S(2)}, u32[]{:S(2)}) collective-permute-start(bf16[1024,512]{1,0:T(8,128)(2,1)S(1)} %copy-done.1), channel_id=1, source_target_pairs={{0,16},{1,17},{2,18},{3,19},{4,20},{5,21},{6,22},{7,23},{8,24},{9,... | collective-permute-start | bytes 3145736 | tf_op jit(solution)/shard_map/ppermute | solution.py:35
  117.3 3.1 %fusion.22 = f32[1024,512]{1,0:T(8,128)} fusion(bf16[1024,512]{1,0:T(8,128)(2,1)S(1)} %copy-done.1, bf16[6,512,512]{2,1,0:T(8,128)(2,1)} %param.5), kind=kOutput, calls=%fused_computation.30 | convolution fusion | flops 536870912 | bytes 3670016 | tf_op jit(solution)/shard_map/dot_general | solution.py:44
  120.4 0.0 collective-permute-done.3
  120.4 0.0 copy-done.2
  120.4 3.3 %fusion.14 = f32[1024,512]{1,0:T(8,128)} fusion(bf16[1024,512]{1,0:T(8,128)(2,1)} %collective-permute-done.3, bf16[6,512,512]{2,1,0:T(8,128)(2,1)S(1)} %copy-done.2), kind=kOutput, calls=%fused_computation.22 | convolution fusion | flops 536870912 | bytes 3670016 | tf_op jit(solution)/shard_map/dot_general | solution.py:47
  123.7 53.6 %collective-permute-done.2 = bf16[1024,512]{1,0:T(8,128)(2,1)S(1)} collective-permute-done((bf16[1024,512]{1,0:T(8,128)(2,1)S(1)}, bf16[1024,512]{1,0:T(8,128)(2,1)S(1)}, u32[]{:S(2)}, u32[]{:S(2)}) %collective-permute-start.2) | collective-permute-done | bytes 1048608 | tf_op jit(solution)/shard_map/ppermute | solution.py:35
  177.3 2.0 fusion.16
  179.3 0.0 collective-permute-done.1
  179.3 2.0 fusion.18
  181.4 0.0 collective-permute-done
  181.4 2.1 fusion.20
  183.4 0.0 all-to-all-done.1
  183.5 0.0 copy-done.4
  183.5 0.7 fusion.31
  184.2 20.5 %collective-permute-done.4 = bf16[1024,512]{1,0:T(8,128)(2,1)} collective-permute-done((bf16[1024,512]{1,0:T(8,128)(2,1)S(1)}, bf16[1024,512]{1,0:T(8,128)(2,1)}, u32[]{:S(2)}, u32[]{:S(2)}) %collective-permute-start.4) | collective-permute-done | bytes 1048608 | tf_op jit(solution)/shard_map/ppermute | solution.py:35
  204.7 0.0 copy-done.3
  204.7 9.3 %fusion.2 = bf16[1024,512]{1,0:T(8,128)(2,1)} fusion(f32[1024,512]{1,0:T(8,128)S(1)} %fusion.31, f32[1024,512]{1,0:T(8,128)} %fusion.14, f32[1024,512]{1,0:T(8,128)} %fusion.16, f32[1024,512]{1,0:T(8,128)} %fusion.18, f32[1024,512]{1,0:T(8,128)S(1)} %copy-done.3, f32[1024,512]{1,0:T(8,128)} %fusion.20, bf16[1024,512]{1,0:T(8,128)(2,1)} %collective-permute-done.4, ...), kind=kOutput, calls=%fused_computation.3 | convolution fusion | flops 574095360 | bytes 15204352 | tf_op jit(solution)/shard_map/dot_general | solution.py:47
  (2 shorter events, 0.0 us)
Async XLA Ops:
  0.0 1.0 copy-start
  4.4 80.8 %all-to-all-start = ((f32[32,1024,16]{1,2,0:T(8,128)}), f32[32,1024,16]{1,2,0:T(8,128)S(1)}, u32[]{:S(2)}, u32[]{:S(2)}) async-start(f32[32,1024,16]{1,2,0:T(8,128)} %bitcast.7), calls=%async_computation | async-start | bytes 4194304 | tf_op jit(solution)/shard_map/all_to_all | solution.py:15
  17.5 103.0 %collective-permute-start.3 = (bf16[1024,512]{1,0:T(8,128)(2,1)}, bf16[1024,512]{1,0:T(8,128)(2,1)}, u32[]{:S(2)}, u32[]{:S(2)}) collective-permute-start(bf16[1024,512]{1,0:T(8,128)(2,1)} %param.4), channel_id=1, source_target_pairs={{0,8},{1,9},{2,10},{3,11},{4,12},{5,13},{6,14},{7,15},{8,0},{9,1},... | collective-permute-start | bytes 3145736 | tf_op jit(solution)/shard_map/ppermute | solution.py:35
  85.3 14.3 %copy-start.1 = (bf16[1024,512]{1,0:T(8,128)(2,1)S(1)}, bf16[1024,512]{1,0:T(8,128)(2,1)}, u32[]{:S(2)}) copy-start(bf16[1024,512]{1,0:T(8,128)(2,1)} %param.4) | copy-start | bytes 3145732
  86.4 97.1 %all-to-all-start.1 = ((bf16[32,1024,16]{1,2,0:T(8,128)(2,1)}), bf16[32,1024,16]{1,2,0:T(8,128)(2,1)S(1)}, u32[]{:S(2)}, u32[]{:S(2)}) async-start(bf16[32,1024,16]{1,2,0:T(8,128)(2,1)} %broadcast_in_dim.3), calls=%async_computation.1 | async-start | bytes 2097152 | tf_op jit(solution)/shard_map/all_to_all | solution.py:27
  99.6 20.8 %copy-start.2 = (bf16[6,512,512]{2,1,0:T(8,128)(2,1)S(1)}, bf16[6,512,512]{2,1,0:T(8,128)(2,1)}, u32[]{:S(2)}) copy-start(bf16[6,512,512]{2,1,0:T(8,128)(2,1)} %param.5) | copy-start | bytes 9437188
  99.7 77.7 %collective-permute-start.2 = (bf16[1024,512]{1,0:T(8,128)(2,1)S(1)}, bf16[1024,512]{1,0:T(8,128)(2,1)S(1)}, u32[]{:S(2)}, u32[]{:S(2)}) collective-permute-start(bf16[1024,512]{1,0:T(8,128)(2,1)S(1)} %copy-done.1), channel_id=1, source_target_pairs={{0,4},{1,5},{2,6},{3,7},{4,0},{5,1},{6,2},{7,3},{8,12},{9,13},{10,... | collective-permute-start | bytes 3145736 | tf_op jit(solution)/shard_map/ppermute | solution.py:35
  102.1 77.3 %collective-permute-start.1 = (bf16[1024,512]{1,0:T(8,128)(2,1)S(1)}, bf16[1024,512]{1,0:T(8,128)(2,1)S(1)}, u32[]{:S(2)}, u32[]{:S(2)}) collective-permute-start(bf16[1024,512]{1,0:T(8,128)(2,1)S(1)} %copy-done.1), channel_id=1, source_target_pairs={{0,2},{1,3},{2,0},{3,1},{4,6},{5,7},{6,4},{7,5},{8,10},{9,11},{10,... | collective-permute-start | bytes 3145736 | tf_op jit(solution)/shard_map/ppermute | solution.py:35
  106.7 74.7 %collective-permute-start = (bf16[1024,512]{1,0:T(8,128)(2,1)S(1)}, bf16[1024,512]{1,0:T(8,128)(2,1)S(1)}, u32[]{:S(2)}, u32[]{:S(2)}) collective-permute-start(bf16[1024,512]{1,0:T(8,128)(2,1)S(1)} %copy-done.1), channel_id=1, source_target_pairs={{0,1},{1,0},{2,3},{3,2},{4,5},{5,4},{6,7},{7,6},{8,9},{9,8},{10,11... | collective-permute-start | bytes 3145736 | tf_op jit(solution)/shard_map/ppermute | solution.py:35
  110.1 94.7 %collective-permute-start.4 = (bf16[1024,512]{1,0:T(8,128)(2,1)S(1)}, bf16[1024,512]{1,0:T(8,128)(2,1)}, u32[]{:S(2)}, u32[]{:S(2)}) collective-permute-start(bf16[1024,512]{1,0:T(8,128)(2,1)S(1)} %copy-done.1), channel_id=1, source_target_pairs={{0,16},{1,17},{2,18},{3,19},{4,20},{5,21},{6,22},{7,23},{8,24},{9,... | collective-permute-start | bytes 3145736 | tf_op jit(solution)/shard_map/ppermute | solution.py:35
  181.4 2.1 copy-start.4
  183.5 21.3 %copy-start.3 = (f32[1024,512]{1,0:T(8,128)S(1)}, f32[1024,512]{1,0:T(8,128)}, u32[]{:S(2)}) copy-start(f32[1024,512]{1,0:T(8,128)} %fusion.22) | copy-start | bytes 6291460
where the time goes:
time: 215 us; the launch traced here: 214 us
  waiting for transfers between devices  138 us (64%)
  starting transfers between devices  48.3 us (22%)
  matrix products  25.8 us (12%)
  local copies, waits for them, and re-layouts  2.16 us (1%)
    ppermute x5, waiting for transfers between devices, from_partner(): lax.ppermute(value, axis, [(i, i ^ 1 << apart) for i in range(lax.axis_si...  74.1 us
    all_to_all x1, waiting for transfers between devices, sent_and_summed(): lax.all_to_all(in_blocks(value, dim, peers), axis, 0, 0, tiled=True)  63.4 us
    ppermute x5, starting transfers between devices, from_partner(): lax.ppermute(value, axis, [(i, i ^ 1 << apart) for i in range(lax.axis_si...  21.9 us
    dot_general x5, matrix products, shards(): jnp.dot(neighbour, butterfly[level + 1], preferred_element_type=jnp.float32)  18.7 us
    all_to_all x1, starting transfers between devices, copy_for_each(): return lax.all_to_all(copies, axis, split_axis=0, concat_axis=0, tiled=True)  13.2 us
    all_to_all x1, starting transfers between devices, sent_and_summed(): lax.all_to_all(in_blocks(value, dim, peers), axis, 0, 0, tiled=True)  13.1 us
  transfers between devices with their start and end apart: 7, of which 3 were waited for; matrix products, arithmetic and copies ran while one was open for 7% of the time, Pallas kernels for 0%

commit v1 on v0

v1 whole, which is shorter than its diff:
```python
import functools

import jax
import jax.numpy as jnp
from jax import lax
from jax.experimental import pallas as pl
from jax.experimental.pallas import tpu as pltpu
from jax.sharding import PartitionSpec as P

CHUNKS = 8
AHEAD = 2
STEPS_AT = {0: ["down1"], 1: ["down2"], 2: ["spread"], 3: ["gather"], 4: ["up0"], 5: ["up1"], 6: ["up2"], 7: ["up3"]}
Z_SENT = {0: 0, 1: 1, 2: 2, 3: 4, 4: 5, 5: 6, 6: 7, 7: 8}
NY, NZ = 8, 4
F32, BF16 = jnp.float32, jnp.bfloat16


def dot(a, b):
    return jnp.dot(a, b, preferred_element_type=F32)


def kernel(tok, bfly, down, up, out,
           x, w, wd, wu, got, acc, part, box, from_low, from_high, mine, shares, share_in, mid, o,
           load_sem, send_own, got_sem, pass_sem, down_send, low_sem, high_sem, spread_send, spread_recv,
           gather_send, gather_recv, up_send_r, up_send_l, up_recv, out_sem):
    rows = tok.shape[0]
    step = rows // CHUNKS
    quarter = rows // NZ
    piece = quarter // NY
    me = lax.axis_index("feat")
    y, z = me // NZ, me % NZ
    c = y % 4
    inner = (c == 1) | (c == 2)
    b0, b1, b2 = y % 2, (y // 2) % 2, y // 4
    y1 = y + 1 - 2 * b0
    y2 = y + 2 - 4 * b1
    y3 = y1 + 2 - 4 * b1
    y6 = y2 + 4 - 8 * b2
    z1 = z + 1 - 2 * (z % 2)
    z2 = z + 2 - 4 * (z // 2)

    def at(yy, zz):
        return {"feat": yy * NZ + zz}

    def remote(src, dst, ssem, rsem, yy, zz):
        return pltpu.make_async_remote_copy(
            src_ref=src, dst_ref=dst, send_sem=ssem, recv_sem=rsem,
            device_id=at(yy, zz), device_id_type=pl.DeviceIdType.MESH)

    loads = [
        pltpu.make_async_copy(tok, x, load_sem.at[0]),
        pltpu.make_async_copy(down, wd, load_sem.at[1]),
        pltpu.make_async_copy(bfly, w, load_sem.at[2]),
        pltpu.make_async_copy(up, wu, load_sem.at[3]),
    ]
    for load in loads:
        load.start()

    barrier = pltpu.get_barrier_semaphore()
    peers = [(lax.rem(y + d, NY), z) for d in range(1, NY)] + [(y, lax.rem(z + d, NZ)) for d in range(1, NZ)]
    for yy, zz in peers:
        pl.semaphore_signal(barrier, inc=1, device_id=at(yy, zz), device_id_type=pl.DeviceIdType.MESH)
    pl.semaphore_wait(barrier, len(peers))

    def chunk(k):
        return pl.ds(k * step, step)

    def own(slot, k, yy, zz):
        return remote(tok.at[chunk(k)], got.at[slot, chunk(k)], send_own.at[slot, k], got_sem.at[slot, k], yy, zz)

    def passed(src, slot, k, yy):
        return remote(got.at[src, chunk(k)], got.at[slot, chunk(k)], pass_sem.at[src, k], got_sem.at[slot, k], yy, z)

    def send_y(k):
        @pl.when(inner)
        def _():
            own(1, k, y2, z).start()
        own(0, k, y1, z).start()

    def send_z(k):
        own(3, k, y, z1).start()
        own(4, k, y, z2).start()

    def wait_got(slot, k):
        own(slot, k, y1, z).wait_recv()

    def share(j):
        return pl.ds(pl.multiple_of(j * quarter, quarter), quarter)

    def toward_high(j):
        return remote(box.at[share(j)], from_low.at[j], down_send.at[j], low_sem.at[j], y, z + 1)

    def toward_low(j):
        return remote(box.at[share(j)], from_high.at[j], down_send.at[j], high_sem.at[j], y, z - 1)

    def down_step(s):
        @pl.when(z <= s)
        def _():
            j = NZ - 1 - s + z

            @pl.when(z > 0)
            def _():
                toward_high(j).wait_recv()
                box[share(j), :] = (part[share(j), :] + from_low[j].astype(F32)).astype(BF16)

            @pl.when(z == 0)
            def _():
                box[share(j), :] = part[share(j), :].astype(BF16)
            toward_high(j).start()

        @pl.when(z >= NZ - 1 - s)
        def _():
            j = s - (NZ - 1) + z

            @pl.when(z < NZ - 1)
            def _():
                toward_low(j).wait_recv()
                box[share(j), :] = (part[share(j), :] + from_high[j].astype(F32)).astype(BF16)

            @pl.when(z == NZ - 1)
            def _():
                box[share(j), :] = part[share(j), :].astype(BF16)
            toward_low(j).start()

    def piece_at(yy):
        return pl.ds(pl.multiple_of(yy * piece, piece), piece)

    def spread_copy(d):
        yy = lax.rem(y + d, NY)
        return remote(shares.at[piece_at(yy)], share_in.at[d - 1], spread_send.at[d - 1], spread_recv.at[d - 1], yy, z)

    def spread():
        mine[...] = part[share(z), :]

        @pl.when(z > 0)
        def _():
            toward_high(z).wait_recv()
            mine[...] += from_low[z].astype(F32)

        @pl.when(z < NZ - 1)
        def _():
            toward_low(z).wait_recv()
            mine[...] += from_high[z].astype(F32)
        shares[...] = mine[...].astype(BF16)
        for d in (4, 3, 5, 2, 6, 1, 7):
            spread_copy(d).start()

    def mid_piece(yy):
        return mid.at[pl.ds(pl.multiple_of(z * quarter + yy * piece, piece), piece)]

    def gather_copy(d):
        return remote(mid_piece(y), mid_piece(y), gather_send.at[d - 1], gather_recv.at[d - 1], lax.rem(y + d, NY), z)

    def gather():
        total = mine[piece_at(y), :]
        for d in range(1, NY):
            spread_copy(d).wait_recv()
            total += share_in[d - 1].astype(F32)
        mid[pl.ds(pl.multiple_of(z * quarter + y * piece, piece), piece), :] = total.astype(BF16)
        for d in (4, 3, 5, 2, 6, 1, 7):
            gather_copy(d).start()

    def up_right(j, s):
        return remote(mid.at[share(j)], mid.at[share(j)], up_send_r.at[s], up_recv.at[j], y, z + 1)

    def up_left(j, s):
        return remote(mid.at[share(j)], mid.at[share(j)], up_send_l.at[s], up_recv.at[j], y, z - 1)

    def up_step(s):
        if s == 0:
            for d in range(1, NY):
                gather_copy(d).wait_recv()
        low, high = z - s, z + s

        @pl.when(low >= 0)
        def _():
            if s:
                up_right(low, 0).wait_recv()
            if s < NZ - 1:
                @pl.when(z < NZ - 1)
                def _():
                    up_right(low, s).start()

        @pl.when(high < NZ)
        def _():
            if s:
                up_left(high, 0).wait_recv()
            if s < NZ - 1:
                @pl.when(z > 0)
                def _():
                    up_left(high, s).start()

    steps = {
        "down1": lambda: down_step(1), "down2": lambda: down_step(2), "spread": spread, "gather": gather,
        "up0": lambda: up_step(0), "up1": lambda: up_step(1), "up2": lambda: up_step(2), "up3": lambda: up_step(3),
    }

    for k in range(AHEAD):
        send_y(k)

    loads[0].wait()
    loads[1].wait()

    @pl.loop(0, NZ)
    def _(j):
        part[share(j), :] = dot(x[share(j), :], wd[...])
    down_step(0)
    loads[2].wait()
    loads[3].wait()

    def turn_b(k):
        wait_got(1, k)
        passed(1, 2, k, y6).start()
        acc[chunk(k), :] = dot(x[chunk(k), :], w[0]) + dot(got[0, chunk(k), :], w[3]) + dot(got[1, chunk(k), :], w[4])

    z_sent = 0
    for t in range(CHUNKS):
        if t + AHEAD < CHUNKS:
            send_y(t + AHEAD)
        wait_got(0, t)

        @pl.when(inner)
        def _():
            passed(0, 1, t, y3).start()
        for name in STEPS_AT.get(t, ()):
            steps[name]()
        for k in range(z_sent, Z_SENT[t]):
            send_z(k)
        z_sent = Z_SENT[t]
        if t:
            turn_b(t - 1)
    turn_b(CHUNKS - 1)

    outs = []
    for k in range(CHUNKS):
        wait_got(3, k)
        wait_got(4, k)
        wait_got(2, k)
        rows_k = chunk(k)
        dense = (acc[rows_k, :] + dot(got[3, rows_k, :], w[1]) + dot(got[4, rows_k, :], w[2])
                 + dot(got[2, rows_k, :], w[5]) + dot(mid[rows_k, :], wu[...]))
        o[rows_k, :] = (0.5 * dense * (1.0 + lax.erf(dense * 0.7071067811865476))).astype(BF16)
        store = pltpu.make_async_copy(o.at[rows_k], out.at[rows_k], out_sem.at[k])
        store.start()
        outs.append(store)

    for k in range(CHUNKS):
        own(0, k, y1, z).wait_send()
        own(3, k, y, z1).wait_send()
        own(4, k, y, z2).wait_send()
        passed(1, 2, k, y6).wait_send()

        @pl.when(inner)
        def _():
            own(1, k, y2, z).wait_send()
            passed(0, 1, k, y3).wait_send()
    for d in range(1, NY):
        spread_copy(d).wait_send()
        gather_copy(d).wait_send()
    for j in range(NZ):
        @pl.when(z != j)
        def _():
            toward_high(j).wait_send()
    for s in range(NZ - 1):
        @pl.when((z - s >= 0) & (z < NZ - 1))
        def _():
            up_right(z, s).wait_send()

        @pl.when((z + s < NZ) & (z > 0))
        def _():
            up_left(z, s).wait_send()
    for store in outs:
        store.wait()


def shards(tokens, butterfly, rank_down, rank_up):
    rows, width = tokens.shape
    rank = rank_down.shape[1]
    quarter = rows // NZ
    piece = quarter // NY
    dma = pltpu.SemaphoreType.DMA
    vmem = pltpu.VMEM
    anywhere = pl.BlockSpec(memory_space=pl.ANY)
    return pl.pallas_call(
        kernel,
        out_shape=jax.ShapeDtypeStruct((rows, width), BF16),
        in_specs=[anywhere] * 4,
        out_specs=anywhere,
        scratch_shapes=[
            vmem((rows, width), BF16),
            vmem(butterfly.shape, BF16),
            vmem(rank_down.shape, BF16),
            vmem(rank_up.shape, BF16),
            vmem((5, rows, width), BF16),
            vmem((rows, width), F32),
            vmem((rows, rank), F32),
            vmem((rows, rank), BF16),
            vmem((NZ, quarter, rank), BF16),
            vmem((NZ, quarter, rank), BF16),
            vmem((quarter, rank), F32),
            vmem((quarter, rank), BF16),
            vmem((NY - 1, piece, rank), BF16),
            vmem((rows, rank), BF16),
            vmem((rows, width), BF16),
            dma((4,)), dma((5, CHUNKS)), dma((5, CHUNKS)), dma((2, CHUNKS)),
            dma((NZ,)), dma((NZ,)), dma((NZ,)), dma((NY - 1,)), dma((NY - 1,)),
            dma((NY - 1,)), dma((NY - 1,)), dma((NZ - 1,)), dma((NZ - 1,)), dma((NZ,)), dma((CHUNKS,)),
        ],
        compiler_params=pltpu.CompilerParams(
            collective_id=0, has_side_effects=True, vmem_limit_bytes=48 * 2**20),
        cost_estimate=pl.CostEstimate(
            flops=2 * rows * width * width * 8, bytes_accessed=6 * 2**20, transcendentals=rows * width),
    )(tokens, butterfly, rank_down, rank_up)


def solution(mesh):
    return jax.shard_map(
        shards,
        mesh=mesh,
        in_specs=(P("tok", "feat"), P(None, None, "feat"), P("feat", None), P(None, "feat")),
        out_specs=P("tok", "feat"),
        check_vma=False,
    )
```

time: 215 us -> 117 us (0.54)
  the two profiles are of different devices: /device:TPU:14 before, /device:TPU:268 now
where the time goes in v1:
time: 117 us; the launch traced here: 116 us
  Pallas kernels  112 us (96%)
  local copies, waits for them, and re-layouts  4.28 us (4%)
    pallas_call x1, Pallas kernels, shards(): pl.pallas_call(kernel, out_shape=jax.ShapeDtypeStruct((rows, width), BF16...  112 us
    unnamed x7, local copies, waits for them, and re-layouts  4.28 us

profile of v1, /device:TPU:268, one launch (start us, length us, event | category | flops | bytes accessed | tf_op | source)
XLA Modules:
  0.0 116.4 jit_solution(479221652978477483)
XLA Ops:
  0.0 0.0 copy-start
  0.0 1.2 %copy-done = bf16[1024,512]{1,0:T(8,128)(2,1)S(1)} copy-done((bf16[1024,512]{1,0:T(8,128)(2,1)S(1)}, bf16[1024,512]{1,0:T(8,128)(2,1)}, u32[]{:S(2)}) %copy-start) | copy-done | bytes 1048600
  1.2 0.0 copy-start.1
  1.2 1.0 copy-done.1
  2.3 0.0 copy-start.2
  2.3 1.0 copy-done.2
  3.3 112.1 %shard_map.46 = bf16[1024,512]{1,0:T(8,128)(2,1)S(1)} custom-call(bf16[1024,512]{1,0:T(8,128)(2,1)S(1)} %copy-done, bf16[6,512,512]{2,1,0:T(8,128)(2,1)} %bfly.1, bf16[512,512]{1,0:T(8,128)(2,1)S(1)} %copy-done.1, bf16[512,512]{1,0:T(8,128)(2,1)S(1)} %copy-done.2), custom_call_target="tpu_custom_call" | custom-call | flops 4294967296 | bytes 6291456 | tf_op jit(solution)/shard_map/pallas_call | solution.py:284
  115.4 1.0 copy.6
Async XLA Ops:
  0.0 1.2 %copy-start = (bf16[1024,512]{1,0:T(8,128)(2,1)S(1)}, bf16[1024,512]{1,0:T(8,128)(2,1)}, u32[]{:S(2)}) copy-start(bf16[1024,512]{1,0:T(8,128)(2,1)} %tok.1) | copy-start | bytes 3145732
  1.2 1.0 copy-start.1
  2.3 1.0 copy-start.2

commit v2 on v1

v2 whole, which is shorter than its diff:
```python
import functools

import jax
import jax.numpy as jnp
from jax import lax
from jax.experimental import pallas as pl
from jax.experimental.pallas import tpu as pltpu
from jax.sharding import PartitionSpec as P

CHUNKS = 8
GROUPS = 2


def plan():
    order = [('y', 0), ('m', 0), ('d', 0), ('d', 1), ('w', 0), ('y', 1), ('a', 0), ('d', 2), ('d', 3), ('z', 0), ('y', 2), ('a', 1), ('b', 0), ('d', 4), ('d', 5), ('z', 1), ('z', 2), ('p', 0), ('y', 3), ('a', 2), ('b', 1), ('h', 0), ('h', 1), ('z', 3), ('z', 4), ('p', 1), ('y', 4), ('a', 3), ('b', 2), ('s', 0), ('s', 1), ('g', 0), ('g', 1), ('z', 5), ('z', 6), ('p', 2), ('y', 5), ('a', 4), ('b', 3), ('j', 0), ('j', 1), ('z', 7), ('p', 3), ('y', 6), ('a', 5), ('b', 4), ('u', 0), ('u', 1), ('p', 4), ('y', 7), ('a', 6), ('b', 5), ('u', 2), ('u', 3), ('p', 5), ('a', 7), ('b', 6), ('u', 4), ('u', 5), ('p', 6), ('b', 7), ('u', 6), ('u', 7), ('p', 7), ('f', 0), ('f', 1), ('f', 2), ('f', 3), ('f', 4), ('f', 5), ('f', 6), ('f', 7)]
    return order


NY, NZ = 8, 4
F32, BF16 = jnp.float32, jnp.bfloat16


def dot(a, b):
    return jnp.dot(a, b, preferred_element_type=F32)


def kernel(tok, bfly, down, up, out,
           x, w, wd, wu, got, acc, part, box, from_low, from_high, mine, shares, pair_in, share_in, mid, o,
           load_sem, send_own, got_sem, pass_sem, down_send, low_sem, high_sem, halve_send, halve_recv, spread_send, spread_recv,
           gather_send, gather_recv, join_send, join_recv, up_send_r, up_send_l, up_recv, out_sem):
    rows = tok.shape[0]
    step = rows // CHUNKS
    quarter = rows // NZ
    part_rows = quarter // GROUPS
    half = part_rows // 2
    piece = part_rows // NY
    me = lax.axis_index("feat")
    y, z = me // NZ, me % NZ
    b0, b1, b2 = y % 2, (y // 2) % 2, y // 4
    y1 = y + 1 - 2 * b0
    y2 = y + 2 - 4 * b1
    y6 = y2 + 4 - 8 * b2
    mate = lax.rem(y + NY - 1 + 2 * b0, NY)
    z1 = z + 1 - 2 * (z % 2)
    z2 = z + 2 - 4 * (z // 2)

    def at(yy, zz):
        return {"feat": yy * NZ + zz}

    def remote(src, dst, ssem, rsem, yy, zz):
        return pltpu.make_async_remote_copy(
            src_ref=src, dst_ref=dst, send_sem=ssem, recv_sem=rsem,
            device_id=at(yy, zz), device_id_type=pl.DeviceIdType.MESH)

    loads = [
        pltpu.make_async_copy(tok, x, load_sem.at[0]),
        pltpu.make_async_copy(down, wd, load_sem.at[1]),
        pltpu.make_async_copy(bfly, w, load_sem.at[2]),
        pltpu.make_async_copy(up, wu, load_sem.at[3]),
    ]
    for load in loads:
        load.start()

    barrier = pltpu.get_barrier_semaphore()
    peers = [(lax.rem(y + d, NY), z) for d in (1, 2, 4, 6, 7)] + [(y, lax.rem(z + d, NZ)) for d in range(1, NZ)]
    for yy, zz in peers:
        pl.semaphore_signal(barrier, inc=1, device_id=at(yy, zz), device_id_type=pl.DeviceIdType.MESH)
    pl.semaphore_wait(barrier, len(peers))

    def chunk(k):
        return pl.ds(k * step, step)

    def own(slot, k, yy, zz):
        return remote(tok.at[chunk(k)], got.at[slot, chunk(k)], send_own.at[slot, k], got_sem.at[slot, k], yy, zz)

    def passed(src, slot, k, yy):
        return remote(got.at[src, chunk(k)], got.at[slot, chunk(k)], pass_sem.at[k], got_sem.at[slot, k], yy, z)

    def send_y(k):
        own(1, k, y2, z).start()
        own(0, k, y1, z).start()

    def send_z(k):
        own(3, k, y, z1).start()
        own(4, k, y, z2).start()

    def wait_got(slot, k):
        own(slot, k, y1, z).wait_recv()

    def share(j, h):
        return pl.ds(pl.multiple_of(j * quarter + h * part_rows, part_rows), part_rows)

    def toward_high(j, h):
        return remote(box.at[share(j, h)], from_low.at[share(j, h)], down_send.at[h, j], low_sem.at[h, j], y, z + 1)

    def toward_low(j, h):
        return remote(box.at[share(j, h)], from_high.at[share(j, h)], down_send.at[h, j], high_sem.at[h, j], y, z - 1)

    def down_step(s, h):
        @pl.when(z <= s)
        def _():
            j = NZ - 1 - s + z

            @pl.when(z > 0)
            def _():
                toward_high(j, h).wait_recv()
                box[share(j, h), :] = (part[share(j, h), :] + from_low[share(j, h), :].astype(F32)).astype(BF16)

            @pl.when(z == 0)
            def _():
                box[share(j, h), :] = part[share(j, h), :].astype(BF16)
            toward_high(j, h).start()

        @pl.when(z >= NZ - 1 - s)
        def _():
            j = s - (NZ - 1) + z

            @pl.when(z < NZ - 1)
            def _():
                toward_low(j, h).wait_recv()
                box[share(j, h), :] = (part[share(j, h), :] + from_high[share(j, h), :].astype(F32)).astype(BF16)

            @pl.when(z == NZ - 1)
            def _():
                box[share(j, h), :] = part[share(j, h), :].astype(BF16)
            toward_low(j, h).start()

    def place(yy):
        return (yy % 2) * half + (yy // 2) * piece

    def piece_at(yy):
        return pl.ds(pl.multiple_of(place(yy), piece), piece)

    def half_at(odd):
        return pl.ds(pl.multiple_of(odd * half, half), half)

    def halve_copy(h):
        return remote(shares.at[h, half_at(1 - b0)], pair_in.at[h], halve_send.at[h], halve_recv.at[h], mate, z)

    def halve(h):
        mine[h] = part[share(z, h), :]

        @pl.when(z > 0)
        def _():
            toward_high(z, h).wait_recv()
            mine[h] += from_low[share(z, h), :].astype(F32)

        @pl.when(z < NZ - 1)
        def _():
            toward_low(z, h).wait_recv()
            mine[h] += from_high[share(z, h), :].astype(F32)
        shares[h, half_at(1 - b0), :] = mine[h, half_at(1 - b0), :].astype(BF16)
        halve_copy(h).start()

    def spread_copy(d, h):
        yy = lax.rem(y + d, NY)
        return remote(shares.at[h, piece_at(yy)], share_in.at[h, d // 2 - 1], spread_send.at[h, d // 2 - 1],
                      spread_recv.at[h, d // 2 - 1], yy, z)

    def spread(h):
        halve_copy(h).wait_recv()
        mine[h, half_at(b0), :] += pair_in[h].astype(F32)
        shares[h, half_at(b0), :] = mine[h, half_at(b0), :].astype(BF16)
        for d in (4, 2, 6):
            spread_copy(d, h).start()

    def mid_rows(start, count, h):
        return pl.ds(pl.multiple_of(z * quarter + h * part_rows + start, piece), count)

    def gather_copy(d, h):
        rows_y = mid_rows(place(y), piece, h)
        return remote(mid.at[rows_y], mid.at[rows_y], gather_send.at[h, d // 2 - 1], gather_recv.at[h, d // 2 - 1],
                      lax.rem(y + d, NY), z)

    def gather(h):
        total = mine[h, piece_at(y), :]
        for d in (2, 4, 6):
            spread_copy(d, h).wait_recv()
            total += share_in[h, d // 2 - 1].astype(F32)
        mid[mid_rows(place(y), piece, h), :] = total.astype(BF16)
        for d in (4, 2, 6):
            gather_copy(d, h).start()

    def join_copy(h):
        rows_half = mid_rows(b0 * half, half, h)
        return remote(mid.at[rows_half], mid.at[rows_half], join_send.at[h], join_recv.at[h], mate, z)

    def join(h):
        for d in (2, 4, 6):
            gather_copy(d, h).wait_recv()
        join_copy(h).start()

    def up_right(j, s, h):
        return remote(mid.at[share(j, h)], mid.at[share(j, h)], up_send_r.at[h, s], up_recv.at[h, j], y, z + 1)

    def up_left(j, s, h):
        return remote(mid.at[share(j, h)], mid.at[share(j, h)], up_send_l.at[h, s], up_recv.at[h, j], y, z - 1)

    def up_step(s, h):
        if s == 0:
            join_copy(h).wait_recv()
        low, high = z - s, z + s

        @pl.when(low >= 0)
        def _():
            if s:
                up_right(low, 0, h).wait_recv()
            if s < NZ - 1:
                @pl.when(z < NZ - 1)
                def _():
                    up_right(low, s, h).start()

        @pl.when(high < NZ)
        def _():
            if s:
                up_left(high, 0, h).wait_recv()
            if s < NZ - 1:
                @pl.when(z > 0)
                def _():
                    up_left(high, s, h).start()

    def pass_a(k):
        wait_got(0, k)

    def pass_b(k):
        wait_got(1, k)
        passed(1, 2, k, y6).start()

    def first_half(k):
        acc[chunk(k), :] = dot(x[chunk(k), :], w[0]) + dot(got[0, chunk(k), :], w[3]) + dot(got[1, chunk(k), :], w[4])

    def project(_):
        loads[0].wait()
        loads[1].wait()

        @pl.loop(0, NZ)
        def _(j):
            rows_j = pl.ds(pl.multiple_of(j * quarter, quarter), quarter)
            part[rows_j, :] = dot(x[rows_j, :], wd[...])

    def weights(_):
        loads[2].wait()
        loads[3].wait()

    outs = []

    def finish(k):
        wait_got(3, k)
        wait_got(4, k)
        wait_got(2, k)
        rows_k = chunk(k)
        dense = (acc[rows_k, :] + dot(got[3, rows_k, :], w[1]) + dot(got[4, rows_k, :], w[2])
                 + dot(got[2, rows_k, :], w[5]) + dot(mid[rows_k, :], wu[...]))
        o[rows_k, :] = (0.5 * dense * (1.0 + lax.erf(dense * 0.7071067811865476))).astype(BF16)
        store = pltpu.make_async_copy(o.at[rows_k], out.at[rows_k], out_sem.at[k])
        store.start()
        outs.append(store)

    steps = {
        "y": send_y, "z": send_z, "a": pass_a, "b": pass_b, "p": first_half, "f": finish,
        "m": project, "w": weights, "h": halve, "s": spread, "g": gather, "j": join,
        "d": lambda i: down_step(i // GROUPS, i % GROUPS), "u": lambda i: up_step(i // GROUPS, i % GROUPS),
    }
    for name, number in plan():
        steps[name](number)

    for k in range(CHUNKS):
        own(0, k, y1, z).wait_send()
        own(3, k, y, z1).wait_send()
        own(4, k, y, z2).wait_send()
        passed(1, 2, k, y6).wait_send()
        own(1, k, y2, z).wait_send()
    for h in range(GROUPS):
        halve_copy(h).wait_send()
        join_copy(h).wait_send()
        for d in (2, 4, 6):
            spread_copy(d, h).wait_send()
            gather_copy(d, h).wait_send()
        for j in range(NZ):
            @pl.when(z != j)
            def _():
                toward_high(j, h).wait_send()
        for s in range(NZ - 1):
            @pl.when((z - s >= 0) & (z < NZ - 1))
            def _():
                up_right(z, s, h).wait_send()

            @pl.when((z + s < NZ) & (z > 0))
            def _():
                up_left(z, s, h).wait_send()
    for store in outs:
        store.wait()


def shards(tokens, butterfly, rank_down, rank_up):
    rows, width = tokens.shape
    rank = rank_down.shape[1]
    quarter = rows // NZ
    part_rows = quarter // GROUPS
    piece = part_rows // NY
    dma = pltpu.SemaphoreType.DMA
    vmem = pltpu.VMEM
    anywhere = pl.BlockSpec(memory_space=pl.ANY)
    return pl.pallas_call(
        kernel,
        out_shape=jax.ShapeDtypeStruct((rows, width), BF16),
        in_specs=[anywhere] * 4,
        out_specs=anywhere,
        scratch_shapes=[
            vmem((rows, width), BF16),
            vmem(butterfly.shape, BF16),
            vmem(rank_down.shape, BF16),
            vmem(rank_up.shape, BF16),
            vmem((5, rows, width), BF16),
            vmem((rows, width), F32),
            vmem((rows, rank), F32),
            vmem((rows, rank), BF16),
            vmem((rows, rank), BF16),
            vmem((rows, rank), BF16),
            vmem((GROUPS, part_rows, rank), F32),
            vmem((GROUPS, part_rows, rank), BF16),
            vmem((GROUPS, part_rows // 2, rank), BF16),
            vmem((GROUPS, 3, piece, rank), BF16),
            vmem((rows, rank), BF16),
            vmem((rows, width), BF16),
            dma((4,)), dma((5, CHUNKS)), dma((5, CHUNKS)), dma((CHUNKS,)),
            dma((GROUPS, NZ)), dma((GROUPS, NZ)), dma((GROUPS, NZ)), dma((GROUPS,)), dma((GROUPS,)), dma((GROUPS, 3)), dma((GROUPS, 3)),
            dma((GROUPS, 3)), dma((GROUPS, 3)), dma((GROUPS,)), dma((GROUPS,)), dma((GROUPS, NZ - 1)), dma((GROUPS, NZ - 1)), dma((GROUPS, NZ)),
            dma((CHUNKS,)),
        ],
        compiler_params=pltpu.CompilerParams(
            collective_id=0, has_side_effects=True, vmem_limit_bytes=63 * 2**20),
        cost_estimate=pl.CostEstimate(
            flops=2 * rows * width * width * 8, bytes_accessed=6 * 2**20, transcendentals=rows * width),
    )(tokens, butterfly, rank_down, rank_up)


def solution(mesh):
    return jax.shard_map(
        shards,
        mesh=mesh,
        in_specs=(P("tok", "feat"), P(None, None, "feat"), P("feat", None), P(None, "feat")),
        out_specs=P("tok", "feat"),
        check_vma=False,
    )
```

time: 117 us -> 99.3 us (0.85)
  the two profiles are of different devices: /device:TPU:268 before, /device:TPU:6 now
where the time goes in v2:
time: 99.3 us; the launch traced here: 99.1 us
  Pallas kernels  96.9 us (98%)
  local copies, waits for them, and re-layouts  2.26 us (2%)
    pallas_call x1, Pallas kernels, shards(): pl.pallas_call(kernel, out_shape=jax.ShapeDtypeStruct((rows, width), BF16...  96.9 us
    unnamed x1, local copies, waits for them, and re-layouts  2.26 us

profile of v2, /device:TPU:6, one launch (start us, length us, event | category | flops | bytes accessed | tf_op | source)
XLA Modules:
  0.0 99.1 jit_solution(17173042676341086129)
XLA Ops:
  0.0 96.9 %shard_map.46 = bf16[1024,512]{1,0:T(8,128)(2,1)} custom-call(bf16[1024,512]{1,0:T(8,128)(2,1)} %tok.1, bf16[6,512,512]{2,1,0:T(8,128)(2,1)} %bfly.1, bf16[512,512]{1,0:T(8,128)(2,1)} %down.1, bf16[512,512]{1,0:T(8,128)(2,1)} %up.1), custom_call_target="tpu_custom_call" | custom-call | flops 4294967296 | bytes 6291456 | tf_op jit(solution)/shard_map/pallas_call | solution.py:304
  96.9 2.3 %copy.6 = bf16[1024,512]{1,0:T(8,128)(2,1)} copy(bf16[1024,512]{1,0:T(8,128)(2,1)} %shard_map.46) | data formatting | bytes 2097152

commit v3 on v2

--- a/solution.py
+++ b/solution.py
@@ -12,7 +12,7 @@
 
 
 def plan():
-    order = [('y', 0), ('m', 0), ('d', 0), ('d', 1), ('w', 0), ('y', 1), ('a', 0), ('d', 2), ('d', 3), ('z', 0), ('y', 2), ('a', 1), ('b', 0), ('d', 4), ('d', 5), ('z', 1), ('z', 2), ('p', 0), ('y', 3), ('a', 2), ('b', 1), ('h', 0), ('h', 1), ('z', 3), ('z', 4), ('p', 1), ('y', 4), ('a', 3), ('b', 2), ('s', 0), ('s', 1), ('g', 0), ('g', 1), ('z', 5), ('z', 6), ('p', 2), ('y', 5), ('a', 4), ('b', 3), ('j', 0), ('j', 1), ('z', 7), ('p', 3), ('y', 6), ('a', 5), ('b', 4), ('u', 0), ('u', 1), ('p', 4), ('y', 7), ('a', 6), ('b', 5), ('u', 2), ('u', 3), ('p', 5), ('a', 7), ('b', 6), ('u', 4), ('u', 5), ('p', 6), ('b', 7), ('u', 6), ('u', 7), ('p', 7), ('f', 0), ('f', 1), ('f', 2), ('f', 3), ('f', 4), ('f', 5), ('f', 6), ('f', 7)]
+    order = [('y', 0), ('m', 0), ('d', 0), ('d', 1), ('w', 0), ('y', 1), ('a', 0), ('d', 2), ('d', 3), ('z', 0), ('b', 0), ('y', 2), ('a', 1), ('d', 4), ('d', 5), ('z', 1), ('z', 2), ('p', 0), ('b', 1), ('y', 3), ('a', 2), ('h', 0), ('h', 1), ('z', 3), ('z', 4), ('p', 1), ('b', 2), ('y', 4), ('a', 3), ('s', 0), ('s', 1), ('g', 0), ('g', 1), ('z', 5), ('z', 6), ('p', 2), ('b', 3), ('y', 5), ('a', 4), ('j', 0), ('j', 1), ('z', 7), ('p', 3), ('b', 4), ('y', 6), ('a', 5), ('u', 0), ('u', 1), ('p', 4), ('y', 7), ('a', 6), ('b', 5), ('u', 2), ('u', 3), ('p', 5), ('a', 7), ('b', 6), ('u', 4), ('u', 5), ('p', 6), ('b', 7), ('u', 6), ('u', 7), ('p', 7), ('f', 0), ('f', 1), ('f', 2), ('f', 3), ('f', 4), ('f', 5), ('f', 6), ('f', 7)]
     return order
 
 
@@ -71,7 +71,7 @@
         return pl.ds(k * step, step)
 
     def own(slot, k, yy, zz):
-        return remote(tok.at[chunk(k)], got.at[slot, chunk(k)], send_own.at[slot, k], got_sem.at[slot, k], yy, zz)
+        return remote(x.at[chunk(k)], got.at[slot, chunk(k)], send_own.at[slot, k], got_sem.at[slot, k], yy, zz)
 
     def passed(src, slot, k, yy):
         return remote(got.at[src, chunk(k)], got.at[slot, chunk(k)], pass_sem.at[k], got_sem.at[slot, k], yy, z)
@@ -230,7 +230,6 @@
         acc[chunk(k), :] = dot(x[chunk(k), :], w[0]) + dot(got[0, chunk(k), :], w[3]) + dot(got[1, chunk(k), :], w[4])
 
     def project(_):
-        loads[0].wait()
         loads[1].wait()
 
         @pl.loop(0, NZ)
@@ -261,6 +260,7 @@
         "m": project, "w": weights, "h": halve, "s": spread, "g": gather, "j": join,
         "d": lambda i: down_step(i // GROUPS, i % GROUPS), "u": lambda i: up_step(i // GROUPS, i % GROUPS),
     }
+    loads[0].wait()
     for name, number in plan():
         steps[name](number)
 

time: 99.3 us -> 99.1 us (level)
  no operation moved by 1% of the time
where the time goes in v3:
time: 99.1 us; the launch traced here: 99 us
  Pallas kernels  96.7 us (98%)
  local copies, waits for them, and re-layouts  2.26 us (2%)
    pallas_call x1, Pallas kernels, shards(): pl.pallas_call(kernel, out_shape=jax.ShapeDtypeStruct((rows, width), BF16...  96.7 us
    unnamed x1, local copies, waits for them, and re-layouts  2.26 us

profile of v3, /device:TPU:6, one launch (start us, length us, event | category | flops | bytes accessed | tf_op | source)
XLA Modules:
  0.0 99.0 jit_solution(15055383708877160072)
XLA Ops:
  0.0 96.7 %shard_map.46 = bf16[1024,512]{1,0:T(8,128)(2,1)} custom-call(bf16[1024,512]{1,0:T(8,128)(2,1)} %tok.1, bf16[6,512,512]{2,1,0:T(8,128)(2,1)} %bfly.1, bf16[512,512]{1,0:T(8,128)(2,1)} %down.1, bf16[512,512]{1,0:T(8,128)(2,1)} %up.1), custom_call_target="tpu_custom_call" | custom-call | flops 4294967296 | bytes 6291456 | tf_op jit(solution)/shard_map/pallas_call | solution.py:304
  96.7 2.3 %copy.6 = bf16[1024,512]{1,0:T(8,128)(2,1)} copy(bf16[1024,512]{1,0:T(8,128)(2,1)} %shard_map.46) | data formatting | bytes 2097152

commit v4 on v3

--- a/solution.py
+++ b/solution.py
@@ -329,7 +329,7 @@
             dma((CHUNKS,)),
         ],
         compiler_params=pltpu.CompilerParams(
-            collective_id=0, has_side_effects=True, vmem_limit_bytes=63 * 2**20),
+            collective_id=0, has_side_effects=True, vmem_limit_bytes=51 * 2**20),
         cost_estimate=pl.CostEstimate(
             flops=2 * rows * width * width * 8, bytes_accessed=6 * 2**20, transcendentals=rows * width),
     )(tokens, butterfly, rank_down, rank_up)

time: 99.1 us -> 101 us (1.019)
  Pallas kernels: 96.7 us -> 97.8 us
    pallas_call x1, Pallas kernels: 96.7 us -> 97.8 us  [shards(): pl.pallas_call(kernel, out_shape=jax.ShapeDtypeStruct((rows, width), BF16...]
    unnamed x1 -> x5, local copies, waits for them, and re-layouts: 2.26 us -> 3.05 us
where the time goes in v4:
time: 101 us
  Pallas kernels  97.8 us (97%)
  local copies, waits for them, and re-layouts  3.05 us (3%)
    pallas_call x1, Pallas kernels, shards(): pl.pallas_call(kernel, out_shape=jax.ShapeDtypeStruct((rows, width), BF16...  97.8 us
    unnamed x5, local copies, waits for them, and re-layouts  3.05 us

profile of v4, /device:TPU:6, one launch (start us, length us, event | category | flops | bytes accessed | tf_op | source)
XLA Modules:
  0.0 100.9 jit_solution(13783074350275379371)
XLA Ops:
  0.0 0.0 copy-start
  0.0 1.0 %copy-done = bf16[512,512]{1,0:T(8,128)(2,1)S(1)} copy-done((bf16[512,512]{1,0:T(8,128)(2,1)S(1)}, bf16[512,512]{1,0:T(8,128)(2,1)}, u32[]{:S(2)}) %copy-start) | copy-done | bytes 524312
  1.0 0.0 copy-start.1
  1.0 1.0 %copy-done.1 = bf16[512,512]{1,0:T(8,128)(2,1)S(1)} copy-done((bf16[512,512]{1,0:T(8,128)(2,1)S(1)}, bf16[512,512]{1,0:T(8,128)(2,1)}, u32[]{:S(2)}) %copy-start.1) | copy-done | bytes 524312
  2.1 97.8 %shard_map.46 = bf16[1024,512]{1,0:T(8,128)(2,1)S(1)} custom-call(bf16[1024,512]{1,0:T(8,128)(2,1)} %tok.1, bf16[6,512,512]{2,1,0:T(8,128)(2,1)} %bfly.1, bf16[512,512]{1,0:T(8,128)(2,1)S(1)} %copy-done, bf16[512,512]{1,0:T(8,128)(2,1)S(1)} %copy-done.1), custom_call_target="tpu_custom_call" | custom-call | flops 4294967296 | bytes 6291456 | tf_op jit(solution)/shard_map/pallas_call | solution.py:304
  99.9 1.0 copy.6
Async XLA Ops:
  0.0 1.0 %copy-start = (bf16[512,512]{1,0:T(8,128)(2,1)S(1)}, bf16[512,512]{1,0:T(8,128)(2,1)}, u32[]{:S(2)}) copy-start(bf16[512,512]{1,0:T(8,128)(2,1)} %down.1) | copy-start | bytes 1572868
  1.0 1.0 %copy-start.1 = (bf16[512,512]{1,0:T(8,128)(2,1)S(1)}, bf16[512,512]{1,0:T(8,128)(2,1)}, u32[]{:S(2)}) copy-start(bf16[512,512]{1,0:T(8,128)(2,1)} %up.1) | copy-start | bytes 1572868
